TPU v7x, 128 devices: a whole 4x4x4 slice. The times are simulated.
128 devices in a mesh: chan: 4 (over y), feed: 32 (over z, x, core).
Axes of the slice: x: 4, y: 4, z: 4, core: 2. Of those that a mesh axis runs over, the one named last changes fastest.
Arguments:
- volt: bfloat16 [2, 1024, 32, 4096], P(None, 'feed', 'chan'), may hold values from -6 to 6
- pulsar_beam: int32 [512], replicated, may hold values from 0 to 1023, as said below
- phase_bin: int32 [512, 32, 4096], P('feed'), may hold values from 0 to 255
Outputs:
- intensity: float32 [1024, 32, 256], P('feed', 'chan')
- folded: float32 [512, 256], P('feed')
Inputs may be any that keep to these rules, and one draw needn't show every extreme that they name: For pulsars n in one block of 16 consecutive indices, the number whose pulsar_beam lies in one block of 32 consecutive rows is 0 or exactly 2.
All inputs are finite; a program needn't handle non-finite values.
Results may differ from a plain program's by a relative error of at most 0.007.
Values may be sent and summed in bfloat16 or wider, within the bound.
A program may use at most 128 MiB of HBM per device.

v0:
```python
import math

import jax
import jax.numpy as jnp
from jax import lax
from jax.sharding import PartitionSpec as P

F = 1024
NBIN = 256
DS = 16
SEND_CAP = 2


def partner_2(block, axis, stride):
    count = lax.axis_size(axis)
    route = []
    for low in range(count):
        high = low | 1 << stride
        if high != low and high < count:
            route += [(low, high), (high, low)]
    return lax.ppermute(block, axis, route)


def reverse_bits(number, bit_count):
    result = jnp.zeros_like(number)
    for shift_bit in range(bit_count):
        result = result + ((number >> shift_bit & 1) << bit_count - 1 - shift_bit)
    return result


def make_weights(beam_group, blocks, per_block, transform_len):
    beam_idx = jnp.arange(per_block, dtype=jnp.int32)[:, None]
    feed_idx = jnp.arange(per_block, dtype=jnp.int32)[None, :]
    phase_step = (
        feed_idx[None] * (beam_group[:, None, None] + blocks * beam_idx[None]) % transform_len
    )
    angle = -2.0 * math.pi * phase_step.astype(jnp.float32) / transform_len
    factor = 1.0 / math.sqrt(transform_len)
    cos_part = (jnp.cos(angle) * factor).astype(jnp.bfloat16)
    sin_part = (jnp.sin(angle) * factor).astype(jnp.bfloat16)
    first = jnp.stack([cos_part, -sin_part], axis=2)
    second = jnp.stack([sin_part, cos_part], axis=2)
    return jnp.stack([first, second], axis=1)


def fold_rows(pulsar_rows, bin_table):
    low_count = 16
    high_count = NBIN // low_count
    high_levels = jnp.arange(high_count, dtype=jnp.int32)[:, None]
    low_levels = jnp.arange(low_count, dtype=jnp.int32)[:, None]

    def fold_one(member):
        series, indices = member
        flat_series = series.reshape(-1)
        flat_bins = indices.reshape(-1)
        high_table = (flat_bins[None, :] // low_count == high_levels).astype(jnp.bfloat16)
        low_table = (flat_bins[None, :] % low_count == low_levels).astype(jnp.bfloat16)
        weighted = high_table * flat_series[None, :]
        grid = lax.dot_general(
            weighted, low_table, (((1,), (1,)), ((), ())), preferred_element_type=jnp.float32
        )
        return grid.reshape(NBIN)

    return lax.map(fold_one, (pulsar_rows, bin_table))


def shards(volt, pulsar_beam, phase_bin):
    blocks = lax.axis_size("feed")
    bit_count = blocks.bit_length() - 1
    per_block = volt.shape[1]
    channels = volt.shape[2]
    samples = volt.shape[3]
    pulsars_here = phase_bin.shape[0]
    position = lax.axis_index("feed")
    signal = volt
    for level_bit in reversed(range(bit_count)):
        half_span = 1 << level_bit
        partner = partner_2(signal, "feed", level_bit)
        is_upper = position >> level_bit & 1
        offset = position & half_span - 1
        angle = -math.pi * offset.astype(jnp.float32) / half_span
        turn_re = jnp.cos(angle)
        turn_im = jnp.sin(angle)
        own_value = signal.astype(jnp.float32)
        far_value = partner.astype(jnp.float32)
        first = jnp.where(is_upper == 1, far_value, own_value)
        second = jnp.where(is_upper == 1, own_value, far_value)
        summed = first + second
        diff_re = first[0] - second[0]
        diff_im = first[1] - second[1]
        differenced = jnp.stack(
            [diff_re * turn_re - diff_im * turn_im, diff_re * turn_im + diff_im * turn_re]
        )
        signal = jnp.where(is_upper == 1, differenced, summed).astype(jnp.bfloat16)
    beam_group = reverse_bits(position[None], bit_count)
    weights = make_weights(beam_group, blocks, per_block, F)[0]
    formed = jnp.einsum(
        "akbl,blct->akct", weights, signal, preferred_element_type=jnp.float32
    ).astype(jnp.bfloat16)
    formed_re = formed[0].astype(jnp.float32)
    formed_im = formed[1].astype(jnp.float32)
    detected = formed_re * formed_re + formed_im * formed_im
    intensity = detected.reshape(per_block, channels, samples // DS, DS).sum(-1) * (1.0 / DS)
    tracks = detected.astype(jnp.bfloat16)
    holder = (pulsar_beam // per_block).reshape(blocks, pulsars_here)
    shared = holder[:, :, None] == holder[:, None, :]
    before = jnp.arange(pulsars_here)[None, :] < jnp.arange(pulsars_here)[:, None]
    ranking = jnp.sum(shared & before[None], axis=2)
    slot_index = (jnp.arange(blocks, dtype=jnp.int32)[:, None] * SEND_CAP + ranking).reshape(-1)
    present = (holder == position).reshape(-1)
    matches = (
        slot_index[None, :] == jnp.arange(blocks * SEND_CAP, dtype=jnp.int32)[:, None]
    ) & present[None, :]
    local_row = jnp.sum(jnp.where(matches, pulsar_beam[None, :] - position * per_block, 0), axis=1)
    filled = jnp.any(matches, axis=1)
    outgoing = jnp.take(tracks, local_row, axis=0)
    outgoing = jnp.where(filled[:, None, None], outgoing, jnp.zeros_like(outgoing))
    received = lax.all_to_all(outgoing, "feed", split_axis=0, concat_axis=0, tiled=True)
    holder_own = lax.dynamic_index_in_dim(holder, position, 0, keepdims=False)
    ranking_own = lax.dynamic_index_in_dim(ranking, position, 0, keepdims=False)
    picked = holder_own * SEND_CAP + ranking_own
    pulsar_rows = jnp.take(received, picked, axis=0)
    channel_total = channels * lax.axis_size("chan")
    all_rows = lax.all_gather(pulsar_rows, "chan", axis=1, tiled=True)
    profile = fold_rows(all_rows, phase_bin)
    folded = profile * (NBIN / (channel_total * samples))
    return (intensity, folded)


def solution(mesh):
    placed = (P(None, "feed", "chan", None), P(), P("feed", None, None))
    return jax.shard_map(
        shards,
        mesh=mesh,
        in_specs=placed,
        out_specs=(P("feed", "chan", None), P("feed", None)),
        check_vma=False,
    )
```

profile of v0, /device:TPU:1, one launch (start us, length us, event | category | flops | bytes accessed | tf_op | source)
XLA Modules:
  0.0 736.4 jit_solution(12135089329036773251)
XLA Ops:
  7.2 4.5 collective-permute-start
  11.8 90.5 %collective-permute-done = bf16[2,32,8,4096]{3,2,1,0:T(8,128)(2,1)} collective-permute-done((bf16[2,32,8,4096]{3,2,1,0:T(8,128)(2,1)}, bf16[2,32,8,4096]{3,2,1,0:T(8,128)(2,1)}, u32[]{:S(2)}, u32[]{:S(2)}) %collective-permute-start) | collective-permute-done | bytes 4194336 | tf_op jit(solution)/shard_map/ppermute | solution.py:21
  102.3 11.6 %convert_select_fusion.9 = (f32[2,32,8,4096]{3,2,1,0:T(8,128)}, f32[2,32,8,4096]{3,2,1,0:T(8,128)}) fusion(bf16[2,32,8,4096]{3,2,1,0:T(8,128)(2,1)} %param.5, bf16[2,32,8,4096]{3,2,1,0:T(8,128)(2,1)} %collective-permute-done, pred[]{:T(512)S(6)} %eq.134), kind=kLoop, calls=%fused_computation.31 | loop fusion | flops 8388608 | bytes 25165824 | tf_op jit(solution)/shard_map/jit(_where)/select_n | solution.py:86
  113.9 6.9 multiply_subtract_fusion.4
  121.0 5.1 fusion.12
  126.9 90.3 %collective-permute-done.1 = bf16[2,32,8,4096]{3,2,1,0:T(8,128)(2,1)} collective-permute-done((bf16[2,32,8,4096]{3,2,1,0:T(8,128)(2,1)}, bf16[2,32,8,4096]{3,2,1,0:T(8,128)(2,1)}, u32[]{:S(2)}, u32[]{:S(2)}) %collective-permute-start.1) | collective-permute-done | bytes 4194336 | tf_op jit(solution)/shard_map/ppermute | solution.py:21
  217.2 11.6 %convert_select_fusion.7 = (f32[2,32,8,4096]{3,2,1,0:T(8,128)}, f32[2,32,8,4096]{3,2,1,0:T(8,128)}) fusion(bf16[2,32,8,4096]{3,2,1,0:T(8,128)(2,1)} %fusion.12, bf16[2,32,8,4096]{3,2,1,0:T(8,128)(2,1)} %collective-permute-done.1, pred[]{:T(512)S(6)} %eq.133), kind=kLoop, calls=%fused_computation.29 | loop fusion | flops 8388608 | bytes 25165824 | tf_op jit(solution)/shard_map/jit(_where)/select_n | solution.py:86
  228.8 6.8 multiply_subtract_fusion.3
  235.6 5.9 fusion.13
  244.4 88.8 %collective-permute-done.2 = bf16[2,32,8,4096]{3,2,1,0:T(8,128)(2,1)} collective-permute-done((bf16[2,32,8,4096]{3,2,1,0:T(8,128)(2,1)}, bf16[2,32,8,4096]{3,2,1,0:T(8,128)(2,1)}, u32[]{:S(2)}, u32[]{:S(2)}) %collective-permute-start.2) | collective-permute-done | bytes 4194336 | tf_op jit(solution)/shard_map/ppermute | solution.py:21
  333.2 11.6 %convert_select_fusion.5 = (f32[2,32,8,4096]{3,2,1,0:T(8,128)}, f32[2,32,8,4096]{3,2,1,0:T(8,128)}) fusion(bf16[2,32,8,4096]{3,2,1,0:T(8,128)(2,1)} %fusion.13, bf16[2,32,8,4096]{3,2,1,0:T(8,128)(2,1)} %collective-permute-done.2, pred[]{:T(512)S(6)} %eq.132), kind=kLoop, calls=%fused_computation.27 | loop fusion | flops 8388608 | bytes 25165824 | tf_op jit(solution)/shard_map/jit(_where)/select_n | solution.py:86
  344.9 6.8 multiply_subtract_fusion.2
  351.6 5.9 fusion.14
  359.4 87.9 %collective-permute-done.3 = bf16[2,32,8,4096]{3,2,1,0:T(8,128)(2,1)} collective-permute-done((bf16[2,32,8,4096]{3,2,1,0:T(8,128)(2,1)}, bf16[2,32,8,4096]{3,2,1,0:T(8,128)(2,1)}, u32[]{:S(2)}, u32[]{:S(2)}) %collective-permute-start.3) | collective-permute-done | bytes 4194336 | tf_op jit(solution)/shard_map/ppermute | solution.py:21
  447.3 11.6 %convert_select_fusion.3 = (f32[2,32,8,4096]{3,2,1,0:T(8,128)}, f32[2,32,8,4096]{3,2,1,0:T(8,128)}) fusion(bf16[2,32,8,4096]{3,2,1,0:T(8,128)(2,1)} %fusion.14, bf16[2,32,8,4096]{3,2,1,0:T(8,128)(2,1)} %collective-permute-done.3, pred[]{:T(512)S(6)} %eq.131), kind=kLoop, calls=%fused_computation.25 | loop fusion | flops 8388608 | bytes 25165824 | tf_op jit(solution)/shard_map/jit(_where)/select_n | solution.py:86
  458.9 6.8 multiply_subtract_fusion.1
  465.7 5.9 fusion.15
  471.6 4.1 collective-permute-start.4
  476.8 6.0 collective-permute-done.4
  482.9 11.6 %convert_select_fusion.1 = (f32[2,32,8,4096]{3,2,1,0:T(8,128)}, f32[2,32,8,4096]{3,2,1,0:T(8,128)}) fusion(bf16[2,32,8,4096]{3,2,1,0:T(8,128)(2,1)} %fusion.15, bf16[2,32,8,4096]{3,2,1,0:T(8,128)(2,1)} %collective-permute-done.4, pred[]{:T(512)S(6)} %eq.130), kind=kLoop, calls=%fused_computation.23 | loop fusion | flops 8388608 | bytes 25165824 | tf_op jit(solution)/shard_map/jit(_where)/select_n | solution.py:86
  494.5 6.6 multiply_subtract_fusion
  501.2 4.6 fusion.16
  505.7 5.6 bitcast_convert_fusion
  511.3 2.9 convert_bitcast_fusion
  518.1 4.0 select_select_fusion
  522.1 6.8 all-to-all-start
  529.1 50.0 %all-to-all-done = bf16[64,8,4096]{2,1,0:T(8,128)(2,1)} async-done(((bf16[64,8,4096]{2,1,0:T(8,128)(2,1)}), bf16[64,8,4096]{2,1,0:T(8,128)(2,1)}, u32[]{:S(2)}, u32[]{:S(2)}) %all-to-all-start) | async-done | bytes 4194336 | tf_op jit(solution)/shard_map/all_to_all | solution.py:118
  579.1 2.8 gather_fusion.1
  583.2 10.4 %copy.23 = f32[1,32,8,4096]{1,3,2,0:T(8,128)} copy(f32[1,32,8,4096]{3,1,2,0:T(8,128)} %get-tuple-element.157) | data formatting | bytes 8388608 | tf_op jit(solution)/shard_map/add | solution.py:102
  593.6 10.3 %reduce_sum.29 = f32[32,8,256]{0,2,1:T(8,128)S(1)} reduce(f32[32,8,256,16]{0,3,2,1:T(8,128)} %bitcast.44, f32[]{:T(128)} %constant.196.clone.1), dimensions={3}, to_apply=%region_0.1 | reduce | flops 983040 | bytes 4456452 | tf_op jit(solution)/shard_map/reduce_sum | solution.py:103
  605.1 26.4 %all-gather.2.cloned.1.call-done = bf16[16,32,4096]{2,1,0:T(8,128)(2,1)} async-done(((bf16[16,8,4096]{2,1,0:T(8,128)(2,1)}), bf16[16,32,4096]{2,1,0:T(8,128)(2,1)}) %all-gather.2.cloned.1.call-update) | async-done | bytes 4194320 | tf_op jit(solution)/shard_map/all_gather | solution.py:124
  631.4 97.3 %while.15 = (s32[]{:T(128)}, f32[16,256]{1,0:T(8,128)S(1)}, s32[16,32,4096]{2,1,0:T(8,128)}, bf16[16,32,4096]{2,1,0:T(8,128)(2,1)}, s32[]{:T(128)}, /*index=5*/s32[]{:T(128)}) while((s32[]{:T(128)}, f32[16,256]{1,0:T(8,128)S(1)}, s32[16,32,4096]{2,1,0:T(8,128)}, bf16[16,32,4096]{2,1,0:T(8,128)(2,1)}, s32[]{:T(128)}, ...), condition=%wide.region_5.6_spmd.clone.clone, body=%wide.region_4.5_spmd.clone.clone.sunk | while | flops 75890688 | bytes 10228817 | solution.py:64
  (183 shorter events, 109.7 us)
Async XLA Ops:
  7.2 95.1 %collective-permute-start = (bf16[2,32,8,4096]{3,2,1,0:T(8,128)(2,1)}, bf16[2,32,8,4096]{3,2,1,0:T(8,128)(2,1)}, u32[]{:S(2)}, u32[]{:S(2)}) collective-permute-start(bf16[2,32,8,4096]{3,2,1,0:T(8,128)(2,1)} %param.5), channel_id=1, source_target_pairs={{0,16},{16,0},{1,17},{17,1},{2,18},{18,2},{3,19},{19,3},{4,20},{20... | collective-permute-start | bytes 12582920 | tf_op jit(solution)/shard_map/ppermute | solution.py:21
  113.9 7.0 copy-start
  126.1 91.2 %collective-permute-start.1 = (bf16[2,32,8,4096]{3,2,1,0:T(8,128)(2,1)}, bf16[2,32,8,4096]{3,2,1,0:T(8,128)(2,1)}, u32[]{:S(2)}, u32[]{:S(2)}) collective-permute-start(bf16[2,32,8,4096]{3,2,1,0:T(8,128)(2,1)} %fusion.12), channel_id=1, source_target_pairs={{0,8},{8,0},{1,9},{9,1},{2,10},{10,2},{3,11},{11,3},{4,12},{12,4},... | collective-permute-start | bytes 12582920 | tf_op jit(solution)/shard_map/ppermute | solution.py:21
  241.5 91.7 %collective-permute-start.2 = (bf16[2,32,8,4096]{3,2,1,0:T(8,128)(2,1)}, bf16[2,32,8,4096]{3,2,1,0:T(8,128)(2,1)}, u32[]{:S(2)}, u32[]{:S(2)}) collective-permute-start(bf16[2,32,8,4096]{3,2,1,0:T(8,128)(2,1)} %fusion.13), channel_id=1, source_target_pairs={{0,4},{4,0},{1,5},{5,1},{2,6},{6,2},{3,7},{7,3},{8,12},{12,8},{9,1... | collective-permute-start | bytes 12582920 | tf_op jit(solution)/shard_map/ppermute | solution.py:21
  357.5 89.8 %collective-permute-start.3 = (bf16[2,32,8,4096]{3,2,1,0:T(8,128)(2,1)}, bf16[2,32,8,4096]{3,2,1,0:T(8,128)(2,1)}, u32[]{:S(2)}, u32[]{:S(2)}) collective-permute-start(bf16[2,32,8,4096]{3,2,1,0:T(8,128)(2,1)} %fusion.14), channel_id=1, source_target_pairs={{0,2},{2,0},{1,3},{3,1},{4,6},{6,4},{5,7},{7,5},{8,10},{10,8},{9,1... | collective-permute-start | bytes 12582920 | tf_op jit(solution)/shard_map/ppermute | solution.py:21
  465.7 10.0 %copy-start.1 = (s32[512]{0:T(512)S(1)}, s32[512]{0:T(512)}, u32[]{:S(2)}) copy-start(s32[512]{0:T(512)} %param.6) | copy-start | bytes 6148
  471.6 11.3 %collective-permute-start.4 = (bf16[2,32,8,4096]{3,2,1,0:T(8,128)(2,1)}, bf16[2,32,8,4096]{3,2,1,0:T(8,128)(2,1)}, u32[]{:S(2)}, u32[]{:S(2)}) collective-permute-start(bf16[2,32,8,4096]{3,2,1,0:T(8,128)(2,1)} %fusion.15), channel_id=1, source_target_pairs={{0,1},{1,0},{2,3},{3,2},{4,5},{5,4},{6,7},{7,6},{8,9},{9,8},{10,11... | collective-permute-start | bytes 12582920 | tf_op jit(solution)/shard_map/ppermute | solution.py:21
  522.1 57.0 %all-to-all-start = ((bf16[64,8,4096]{2,1,0:T(8,128)(2,1)}), bf16[64,8,4096]{2,1,0:T(8,128)(2,1)}, u32[]{:S(2)}, u32[]{:S(2)}) async-start(bf16[64,8,4096]{2,1,0:T(8,128)(2,1)} %select_select_fusion), calls=%async_computation | async-start | bytes 8388608 | tf_op jit(solution)/shard_map/all_to_all | solution.py:118
  528.9 102.6 %all-gather.2.cloned.1.call-start = ((), (), s32[]{:S(2)}) async-start(), calls=%async_computation.1 | async-start | bytes 5242880 | tf_op jit(solution)/shard_map/all_gather | solution.py:124
Sparse Core Ops, SparseCore 0:
  583.3 48.0 all-gather.1
where the time goes:
time: 746 us; the launch traced here: 736 us
  waiting for transfers between devices  440 us (59%)
  other arithmetic  164 us (22%)
  local copies, waits for them, and re-layouts  55.6 us (7%)
  matrix products  40.4 us (5%)
  starting transfers between devices  20.5 us (3%)
  between operations  15.1 us (2%)
    ppermute x5, waiting for transfers between devices, partner_2(): return lax.ppermute(block, axis, route)  364 us
    select_n x5, other arithmetic, shards(): first = jnp.where(is_upper == 1, far_value, own_value)  58.2 us
    all_to_all x1, waiting for transfers between devices, shards(): lax.all_to_all(outgoing, 'feed', split_axis=0, concat_axis=0, tiled=True)  50 us
    while x64, local copies, waits for them, and re-layouts  35.1 us
    dot_general x16, matrix products, fold_one(): lax.dot_general(weighted, low_table, (((1,), (1,)), ((), ())), preferred_...  34.8 us
    sub x5, other arithmetic, shards(): diff_re * turn_re - diff_im * turn_im  33.9 us
    convert_element_type x5, other arithmetic, shards(): signal = jnp.where(is_upper == 1, differenced, summed).astype(jnp.bfloat16)  27.3 us
    all_gather x1, waiting for transfers between devices, shards(): all_rows = lax.all_gather(pulsar_rows, 'chan', axis=1, tiled=True)  26.4 us
  transfers between devices with their start and end apart: 7, of which 7 were waited for; matrix products, arithmetic and copies ran while one was open for 3% of the time, Pallas kernels for 0%

commit v1 on v0

v1 whole, which is shorter than its diff:
```python
import functools
import math

import jax
import jax.numpy as jnp
import ml_dtypes
import numpy as np
from jax import lax
from jax.experimental import pallas as pl
from jax.experimental.pallas import tpu as pltpu
from jax.sharding import PartitionSpec as P

F = 1024
NBIN = 256
DS = 16
BLK = 32
CHD = 8
TD = 128
NP = 8
CUT = 4
PIECE = 16 // CUT
CUT2 = 4
PIECE2 = NP // CUT2
MESH = pl.DeviceIdType.MESH
F32 = jnp.float32
BF16 = jnp.bfloat16


def reverse_bits(number, bit_count):
    return sum((number >> b & 1) << bit_count - 1 - b for b in range(bit_count))


def tables():
    idx = np.arange(BLK)
    rev = np.array([reverse_bits(i, 5) for i in range(BLK)])

    def spread(out_idx):
        angle = 2.0 * math.pi * (np.outer(out_idx, idx) % BLK) / BLK
        cos, sin = np.cos(angle), np.sin(angle)
        parts = np.array([[cos, sin], [-sin, cos]])
        return parts

    eye = np.eye(CHD)
    first = np.einsum("aboi,cd->aocibd", spread(rev), eye).reshape(512, 512)
    second = np.einsum("aboi,cd->aocbid", spread(idx), eye).reshape(512, 512)
    step = np.exp(-2j * math.pi * rev / F)
    step = np.stack([step.real, step.imag])[:, :, None, None] * np.ones((1, 1, CHD, TD))
    avg = np.zeros((8, 2, TD, 8, 2, TD // DS))
    for j in range(8):
        for b in range(2):
            for t in range(TD):
                avg[j, b, t, j, b, t // DS] = 1.0 / DS
    avg = avg.reshape(8, 2 * TD, TD)
    bf = ml_dtypes.bfloat16
    return first.astype(bf), second.astype(bf), step.astype(np.float32), avg.astype(bf)


def routes():
    found = []
    for dz in (0, 1, 3, 2):
        for dx in (0, 1, 3, 2):
            for dc in (0, 1):
                if (dz, dx, dc) != (0, 0, 0):
                    found.append((dz, dx, dc))
    hops = {0: 0, 1: 1, 3: 1, 2: 2}
    found.sort(key=lambda r: -(hops[r[0]] + hops[r[1]]))
    return found


def kernel(
    volt,
    beam,
    phase,
    first_in,
    second_in,
    step_in,
    avg_in,
    inten_out,
    folded_out,
    recv,
    mid,
    det,
    tracks,
    rtracks,
    inten,
    rinten,
    acc,
    bins,
    high,
    low,
    grid,
    rows,
    part,
    parts,
    first,
    second,
    step,
    avg,
    turn,
    local_sem,
    send_sem,
    recv_sem,
    send2_sem,
    recv2_sem,
    send3_sem,
    recv3_sem,
    send4_sem,
    recv4_sem,
):
    me = lax.axis_index("feed")
    chan = lax.axis_index("chan")
    core = me % 2
    x = me // 2 % 4
    z = me // 8

    def towards(route):
        dz, dx, dc = route
        return (((z + dz) % 4) * 4 + (x + dx) % 4) * 2 + (core + dc) % 2

    barrier = pltpu.get_barrier_semaphore()
    for route in routes():
        pl.semaphore_signal(
            barrier, inc=1, device_id=(chan, towards(route)), device_id_type=MESH
        )
    for dy in range(1, 4):
        pl.semaphore_signal(
            barrier, inc=1, device_id=((chan + dy) % 4, me), device_id_type=MESH
        )
    own = pltpu.make_async_copy(
        volt.at[:, :, :, pl.ds(pl.multiple_of(me * TD, TD), TD)], recv.at[me], local_sem.at[0]
    )
    own.start()
    loads = [
        pltpu.make_async_copy(first_in, first, local_sem.at[1]),
        pltpu.make_async_copy(step_in, step, local_sem.at[2]),
        pltpu.make_async_copy(
            phase.at[:, pl.ds(pl.multiple_of(chan * CHD, CHD), CHD), :], bins, local_sem.at[3]
        ),
        pltpu.make_async_copy(second_in, second, local_sem.at[4]),
        pltpu.make_async_copy(avg_in, avg, local_sem.at[5]),
    ]
    pl.semaphore_wait(barrier, 34)

    def send_piece(c, carry):
        for route in routes():
            there = towards(route)
            pltpu.make_async_remote_copy(
                src_ref=volt.at[
                    :, pl.ds(c * PIECE, PIECE), :, pl.ds(pl.multiple_of(there * TD, TD), TD)
                ],
                dst_ref=recv.at[me, :, pl.ds(c * PIECE, PIECE)],
                send_sem=send_sem,
                recv_sem=recv_sem.at[c],
                device_id=(chan, there),
                device_id_type=MESH,
            ).start()
        return carry

    lax.fori_loop(0, CUT, send_piece, 0)
    for load in loads:
        load.start()

    loads[2].wait()

    def digits(n, carry):
        pair = jnp.concatenate([bins[n], bins[n + NP]], axis=0)
        high[n] = (pair >> 4).astype(F32).astype(BF16)
        low[n] = (pair & 15).astype(F32).astype(BF16)
        return carry

    lax.fori_loop(0, NP, digits, 0)
    acc[...] = jnp.zeros_like(acc)
    turn[0] = jnp.full((BLK, CHD, TD), 1.0 / 32.0, F32)
    turn[1] = jnp.zeros((BLK, CHD, TD), F32)
    loads[0].wait()
    loads[1].wait()
    own.wait()

    def section(i, carry):
        both = recv[:, :, i].astype(F32).reshape(2 * BLK, 2, CHD, TD)
        operand = jnp.concatenate(
            [both[:, 0].reshape(512, TD), both[:, 1].reshape(512, TD)], axis=1
        ).astype(BF16)
        result = jnp.dot(first[...], operand, preferred_element_type=F32)
        done = []
        for e in range(2):
            value = result[:, e * TD : (e + 1) * TD].reshape(2, BLK, CHD, TD)
            tr, ti = turn[0], turn[1]
            done.append((value[0] * tr - value[1] * ti, value[0] * ti + value[1] * tr))
            sr, si = step[0], step[1]
            turn[0] = tr * sr - ti * si
            turn[1] = tr * si + ti * sr
        for a in range(2):
            mid[:, a, i] = (
                jnp.concatenate([done[0][a], done[1][a]], axis=1).astype(BF16)
            )
        return carry

    for c in range(CUT):
        span = recv.at[pl.ds(0, BLK - 1), :, pl.ds(c * PIECE, PIECE)]
        pltpu.make_async_copy(span, span, recv_sem.at[c]).wait()
        lax.fori_loop(c * PIECE, (c + 1) * PIECE, section, 0)

    loads[3].wait()
    loads[4].wait()

    def form(j, carry):
        operand = jnp.concatenate(
            [mid[2 * j].reshape(512, TD), mid[2 * j + 1].reshape(512, TD)], axis=1
        )
        result = jnp.dot(second[...], operand, preferred_element_type=F32)
        power = result[:256] * result[:256] + result[256:] * result[256:]
        det[pl.ds(2 * j * BLK, BLK)] = power[:, :TD].reshape(BLK, CHD, TD)
        det[pl.ds((2 * j + 1) * BLK, BLK)] = power[:, TD:].reshape(BLK, CHD, TD)
        acc[j // 8] += jnp.dot(power.astype(BF16), avg[j % 8], preferred_element_type=F32)
        return carry

    lax.fori_loop(0, BLK // 2, form, 0)

    def pick(d, carry):
        for n in range(NP):
            lo_row = det[beam[d * 2 * NP + n]]
            hi_row = det[beam[d * 2 * NP + NP + n]]
            tracks[d, n] = jnp.concatenate([lo_row, hi_row], axis=0).astype(BF16)
        return carry

    lax.fori_loop(0, BLK, pick, 0)
    rtracks[me] = tracks[me]

    def send_tracks(c, carry):
        for route in routes():
            there = towards(route)
            pltpu.make_async_remote_copy(
                src_ref=tracks.at[there, pl.ds(c * PIECE2, PIECE2)],
                dst_ref=rtracks.at[me, pl.ds(c * PIECE2, PIECE2)],
                send_sem=send2_sem,
                recv_sem=recv2_sem.at[c],
                device_id=(chan, there),
                device_id_type=MESH,
            ).start()
        return carry

    lax.fori_loop(0, CUT2, send_tracks, 0)
    for half in range(2):
        inten[pl.ds(16 * half, 16)] = acc[half].T.reshape(16, TD // DS, 256)
    rinten[me] = inten[me]
    for route in routes():
        there = towards(route)
        pltpu.make_async_remote_copy(
            src_ref=inten.at[there],
            dst_ref=rinten.at[me],
            send_sem=send3_sem,
            recv_sem=recv3_sem,
            device_id=(chan, there),
            device_id_type=MESH,
        ).start()

    same = (
        lax.broadcasted_iota(jnp.int32, (256, 256), 0) % 16
        == lax.broadcasted_iota(jnp.int32, (256, 256), 1) % 16
    )
    zero = jnp.zeros((16, TD), BF16)
    one = jnp.ones((16, TD), BF16)

    def fold(n, carry):
        grid[...] = jnp.zeros_like(grid)

        def fold_part(s, carry):
            left, right = [], []
            for e in range(8):
                series = rtracks[s * 8 + e, n]
                span = pl.ds(pl.multiple_of((s * 8 + e) * TD, TD), TD)
                low_now = low[n, :, span]
                high_now = high[n, :, span]
                left.append(
                    jnp.concatenate(
                        [jnp.where(low_now == v, series, zero) for v in range(16)], axis=0
                    )
                )
                right.append(
                    jnp.concatenate(
                        [jnp.where(high_now == v, one, zero) for v in range(16)], axis=0
                    )
                )
            grid[...] += lax.dot_general(
                jnp.concatenate(left, axis=1),
                jnp.concatenate(right, axis=1),
                (((1,), (1,)), ((), ())),
                preferred_element_type=F32,
            )
            return carry

        lax.fori_loop(0, 4, fold_part, 0)
        kept = jnp.where(same, grid[...], 0.0).reshape(BLK, CHD, 256)
        rows[:, pl.ds(n, 1), :] = jnp.sum(kept, axis=1, keepdims=True)
        return carry

    for c in range(CUT2):
        span = rtracks.at[pl.ds(0, BLK - 1), pl.ds(c * PIECE2, PIECE2)]
        pltpu.make_async_copy(span, span, recv2_sem.at[c]).wait()
        lax.fori_loop(c * PIECE2, (c + 1) * PIECE2, fold, 0)

    lane = lax.broadcasted_iota(jnp.int32, (1, 1, 256), 2)
    level = rows[...]
    for d in (8, 4, 2, 1):
        count = 2 * d
        upper = (lane // d) % 2 == 1
        lower_part, upper_part = level[:count], level[count:]
        stay = jnp.where(upper, upper_part, lower_part)
        move = jnp.where(upper, lower_part, upper_part)
        flat = move.reshape(count * NP, 256)
        down = pltpu.roll(flat, d, 1).reshape(count, NP, 256)
        up = pltpu.roll(flat, 256 - d, 1).reshape(count, NP, 256)
        level = stay + jnp.where(upper, down, up)
    part[...] = level.reshape(2 * NP, 256) * (NBIN / (4 * CHD * 4096.0))
    for dy in range(1, 4):
        pltpu.make_async_remote_copy(
            src_ref=part,
            dst_ref=parts.at[dy - 1],
            send_sem=send4_sem,
            recv_sem=recv4_sem.at[dy - 1],
            device_id=((chan + dy) % 4, me),
            device_id_type=MESH,
        ).start()

    span = rinten.at[pl.ds(0, BLK - 1)]
    pltpu.make_async_copy(span, span, recv3_sem).wait()
    inten_out[...] = rinten[...].reshape(256, 256).T.reshape(BLK, CHD, 256)
    for dy in range(1, 4):
        pltpu.make_async_copy(part, parts.at[dy - 1], recv4_sem.at[dy - 1]).wait()
    folded_out[...] = part[...] + parts[0] + parts[1] + parts[2]

    span = recv.at[pl.ds(0, BLK - 1)]
    pltpu.make_async_copy(span, span, send_sem).wait()
    span = rtracks.at[pl.ds(0, BLK - 1)]
    pltpu.make_async_copy(span, span, send2_sem).wait()
    span = rinten.at[pl.ds(0, BLK - 1)]
    pltpu.make_async_copy(span, span, send3_sem).wait()
    pltpu.make_async_copy(parts, parts, send4_sem).wait()


def shards(volt, pulsar_beam, phase_bin):
    first, second, step, avg = tables()
    anywhere = pl.BlockSpec(memory_space=pl.ANY)
    whole = pl.BlockSpec(memory_space=pltpu.VMEM)
    dma = pltpu.SemaphoreType.DMA
    return pl.pallas_call(
        kernel,
        out_shape=(
            jax.ShapeDtypeStruct((BLK, CHD, 4096 // DS), F32),
            jax.ShapeDtypeStruct((2 * NP, NBIN), F32),
        ),
        in_specs=[anywhere, pl.BlockSpec(memory_space=pltpu.SMEM)] + [anywhere] * 5,
        out_specs=(whole, whole),
        scratch_shapes=[
            pltpu.VMEM((BLK, 2, 16, 16, TD), BF16),
            pltpu.VMEM((BLK, 2, 16, 16, TD), BF16),
            pltpu.VMEM((F, CHD, TD), F32),
            pltpu.VMEM((BLK, NP, 16, TD), BF16),
            pltpu.VMEM((BLK, NP, 16, TD), BF16),
            pltpu.VMEM((BLK, TD // DS, 256), F32),
            pltpu.VMEM((BLK, TD // DS, 256), F32),
            pltpu.VMEM((2, 256, TD), F32),
            pltpu.VMEM((2 * NP, CHD, 4096), jnp.int32),
            pltpu.VMEM((NP, 16, 4096), BF16),
            pltpu.VMEM((NP, 16, 4096), BF16),
            pltpu.VMEM((256, 256), F32),
            pltpu.VMEM((BLK, NP, 256), F32),
            pltpu.VMEM((2 * NP, 256), F32),
            pltpu.VMEM((3, 2 * NP, 256), F32),
            pltpu.VMEM((512, 512), BF16),
            pltpu.VMEM((512, 512), BF16),
            pltpu.VMEM((2, BLK, CHD, TD), F32),
            pltpu.VMEM((8, 2 * TD, TD), BF16),
            pltpu.VMEM((2, BLK, CHD, TD), F32),
            dma((6,)),
            dma(()),
            dma((CUT,)),
            dma(()),
            dma((CUT2,)),
            dma(()),
            dma(()),
            dma(()),
            dma((3,)),
        ],
        compiler_params=pltpu.CompilerParams(
            collective_id=0, has_side_effects=True, vmem_limit_bytes=50 * 1024 * 1024
        ),
        name="beams",
    )(
        volt.reshape(2, 16, 16, 4096),
        pulsar_beam,
        phase_bin,
        jnp.asarray(first),
        jnp.asarray(second),
        jnp.asarray(step),
        jnp.asarray(avg),
    )


def solution(mesh):
    placed = (P(None, "feed", "chan", None), P(), P("feed", None, None))
    return jax.shard_map(
        shards,
        mesh=mesh,
        in_specs=placed,
        out_specs=(P("feed", "chan", None), P("feed", None)),
        check_vma=False,
    )
```

time: 746 us -> 95.6 us (0.13); the launches traced: 736 us -> 95.3 us
  waiting for transfers between devices: 440 us -> 0 us
  other arithmetic: 164 us -> 0 us
  Pallas kernels: 0 us -> 88.6 us
  local copies, waits for them, and re-layouts: 55.6 us -> 6.06 us
  matrix products: 40.4 us -> 0 us
  starting transfers between devices: 20.5 us -> 0 us
  between operations: 15.1 us -> 0.65 us
    ppermute x5 -> x0, waiting for transfers between devices: 364 us -> none  [partner_2(): return lax.ppermute(block, axis, route)]
    pallas_call x0 -> x1, Pallas kernels: none -> 88.6 us  [shards(): pl.pallas_call(kernel, out_shape=(jax.ShapeDtypeStruct((BLK, CHD, 4096 //...]
    select_n x25 -> x0, other arithmetic: 70.5 us -> none  [the longest x5 58.2 us: shards(): first = jnp.where(is_upper == 1, far_value, own_value)]
    all_to_all x1 -> x0, waiting for transfers between devices: 50 us -> none  [shards(): lax.all_to_all(outgoing, 'feed', split_axis=0, concat_axis=0, tiled=True)]
    dot_general x17 -> x0, matrix products: 40.4 us -> none  [the longest x16 34.8 us: fold_one(): lax.dot_general(weighted, low_table, (((1,), (1,)), ((), ())), preferred_...]
    while x64 -> x0, local copies, waits for them, and re-layouts: 35.1 us -> none
    sub x6 -> x0, other arithmetic: 33.9 us -> none  [the longest x5 33.9 us: shards(): diff_re * turn_re - diff_im * turn_im]
    convert_element_type x7 -> x0, other arithmetic: 30.4 us -> none  [the longest x5 27.3 us: shards(): signal = jnp.where(is_upper == 1, differenced, summed).astype(jnp.bfloat16)]
  transfers between devices with their start and end apart: 7 -> 0, of which waited for: 7 -> 0; matrix products, arithmetic and copies ran while one was open for 3% -> 0% of each run, Pallas kernels for 0% -> 0%
where the time goes in v1:
time: 95.6 us; the launch traced here: 95.3 us
  Pallas kernels  88.6 us (93%)
  local copies, waits for them, and re-layouts  6.06 us (6%)
    pallas_call x1, Pallas kernels, shards(): pl.pallas_call(kernel, out_shape=(jax.ShapeDtypeStruct((BLK, CHD, 4096 //...  88.6 us
    unnamed x12, local copies, waits for them, and re-layouts  6.06 us

profile of v1, /device:TPU:1, one launch (start us, length us, event | category | flops | bytes accessed | tf_op | source)
XLA Modules:
  0.0 95.3 jit_solution(14834455038818161022)
XLA Ops:
  0.6 0.0 copy-start
  0.6 1.0 %copy-done = bf16[8,256,128]{2,1,0:T(8,128)(2,1)S(1)} copy-done((bf16[8,256,128]{2,1,0:T(8,128)(2,1)S(1)}, bf16[8,256,128]{2,1,0:T(8,128)(2,1)}, u32[]{:S(2)}) %copy-start) | copy-done | bytes 524312
  1.7 0.0 copy-start.1
  1.7 1.0 %copy-done.1 = bf16[512,512]{1,0:T(8,128)(2,1)S(1)} copy-done((bf16[512,512]{1,0:T(8,128)(2,1)S(1)}, bf16[512,512]{1,0:T(8,128)(2,1)}, u32[]{:S(2)}) %copy-start.1) | copy-done | bytes 524312
  2.7 0.0 copy-start.2
  2.7 1.0 %copy-done.2 = bf16[512,512]{1,0:T(8,128)(2,1)S(1)} copy-done((bf16[512,512]{1,0:T(8,128)(2,1)S(1)}, bf16[512,512]{1,0:T(8,128)(2,1)}, u32[]{:S(2)}) %copy-start.2) | copy-done | bytes 524312
  3.8 0.0 copy-start.3
  3.8 0.9 copy-done.3
  4.7 0.0 copy-start.4
  4.7 0.7 copy-done.4
  5.4 88.6 %beams.1 = (f32[32,8,256]{2,1,0:T(8,128)S(1)}, f32[16,256]{1,0:T(8,128)S(1)}) custom-call(bf16[2,16,16,4096]{3,2,1,0:T(8,128)(2,1)} %bitcast.1, s32[512]{0:T(512)S(1)} %copy-done.4, s32[16,32,4096]{2,1,0:T(8,128)} %phase.1, bf16[512,512]{1,0:T(8,128)(2,1)S(1)} %copy-done.2, bf16[512,512]{1,0:T(8,128)(2,1)S(1)} %copy-done.1, f32[2,32,8,128]{3,2,1,0:T(8,128)S(1)} %copy-done.3, ...), custom_call_target="tpu_custom_call" | custom-call | tf_op jit(solution)/shard_map/beams/pallas_call | solution.py:347
  94.0 0.7 copy.11
  94.7 0.6 copy.12
Async XLA Ops:
  0.6 1.0 %copy-start = (bf16[8,256,128]{2,1,0:T(8,128)(2,1)S(1)}, bf16[8,256,128]{2,1,0:T(8,128)(2,1)}, u32[]{:S(2)}) copy-start(bf16[8,256,128]{2,1,0:T(8,128)(2,1)} %constant.11.clone.avg_in) | copy-start | bytes 1572868
  1.7 1.0 %copy-start.1 = (bf16[512,512]{1,0:T(8,128)(2,1)S(1)}, bf16[512,512]{1,0:T(8,128)(2,1)}, u32[]{:S(2)}) copy-start(bf16[512,512]{1,0:T(8,128)(2,1)} %constant.9.clone.second_in) | copy-start | bytes 1572868
  2.7 1.0 %copy-start.2 = (bf16[512,512]{1,0:T(8,128)(2,1)S(1)}, bf16[512,512]{1,0:T(8,128)(2,1)}, u32[]{:S(2)}) copy-start(bf16[512,512]{1,0:T(8,128)(2,1)} %constant.8.clone.first_in) | copy-start | bytes 1572868
  3.8 0.9 copy-start.3
  4.7 0.7 copy-start.4

commit v2 on v1

v2 whole, which is shorter than its diff:
```python
import math

import jax
import jax.numpy as jnp
import ml_dtypes
import numpy as np
from jax import lax
from jax.experimental import pallas as pl
from jax.experimental.pallas import tpu as pltpu
from jax.sharding import PartitionSpec as P

F = 1024
NBIN = 256
DS = 16
TIME = 4096
BLK = 32
CHD = 8
TD = 128
PSR = 16
NQ = 4
PAIRS = 16
CUT = 4
PIECE = PAIRS // CUT
CUT2 = 2
PIECE2 = NQ // CUT2
SUMS = TD // DS
MESH = pl.DeviceIdType.MESH
F32 = jnp.float32
BF16 = jnp.bfloat16


def reverse_bits(number, bit_count):
    return sum((number >> b & 1) << bit_count - 1 - b for b in range(bit_count))


def tables():
    idx = np.arange(BLK)
    rev = np.array([reverse_bits(i, 5) for i in range(BLK)])

    def transform(out_idx):
        angle = 2.0 * math.pi * (np.outer(out_idx, idx) % BLK) / BLK
        cos, sin = np.cos(angle), np.sin(angle)
        return np.array([[cos, sin], [-sin, cos]])

    first = np.einsum("aboi,cd->aocibd", transform(rev), np.eye(8)).reshape(512, 512)
    within = transform(idx).reshape(2, 2, BLK, PAIRS, 2)
    second = np.einsum("aboij,cd->aocibjd", within, np.eye(4)).reshape(256, 256)
    step = np.exp(-2j * math.pi * 2 * rev / F)[:, None] * np.ones((1, 8))
    start = np.exp(-2j * math.pi * np.outer(rev, np.arange(8) // 4) / F) / 32.0
    turns = np.stack([step.real, step.imag, start.real, start.imag])
    turns = turns[..., None] * np.ones(TD)
    avg = np.zeros((4, 4, TD, 16, SUMS))
    for j in range(4):
        for b in range(4):
            for t in range(TD):
                avg[j, b, t, 4 * j + b, t // DS] = 1.0 / DS
    avg = avg.reshape(4, 4 * TD, TD)
    bf = ml_dtypes.bfloat16
    return first.astype(bf), second.astype(bf), turns.astype(np.float32), avg.astype(bf)


def routes():
    hops = {0: 0, 1: 1, 3: 1, 2: 2}
    found = [
        (dz, dx, dc)
        for dz in (0, 1, 3, 2)
        for dx in (0, 1, 3, 2)
        for dc in (0, 1)
        if (dz, dx, dc) != (0, 0, 0)
    ]
    found.sort(key=lambda r: -(hops[r[0]] + hops[r[1]]))
    return found


def halves(low_rows, high_rows):
    upper = lax.broadcasted_iota(jnp.int32, low_rows.shape, low_rows.ndim - 2) >= 4
    axis = low_rows.ndim - 2
    return (
        jnp.where(upper, pltpu.roll(high_rows, 4, axis), low_rows),
        jnp.where(upper, high_rows, pltpu.roll(low_rows, 4, axis)),
    )


def kernel(
    volt,
    beam_in,
    phase,
    first_in,
    second_in,
    turns_in,
    avg_in,
    inten_out,
    folded_out,
    held,
    sent,
    recv,
    mid,
    det,
    tracks,
    rtracks,
    inten,
    rinten,
    acc,
    bins,
    high,
    low,
    grid,
    part,
    parts,
    first,
    second,
    turns,
    avg,
    turn,
    beam,
    local_sem,
    held_sem,
    send_sem,
    recv_sem,
    send2_sem,
    recv2_sem,
    send3_sem,
    recv3_sem,
    send4_sem,
    recv4_sem,
):
    me = lax.axis_index("feed")
    chan = lax.axis_index("chan")
    core = me % 2
    x = me // 2 % 4
    z = me // 8

    def towards(route):
        dz, dx, dc = route
        return (((z + dz) % 4) * 4 + (x + dx) % 4) * 2 + (core + dc) % 2

    barrier = pltpu.get_barrier_semaphore()
    for route in routes():
        pl.semaphore_signal(
            barrier, inc=1, device_id=(chan, towards(route)), device_id_type=MESH
        )
    for dy in range(1, 4):
        pl.semaphore_signal(
            barrier, inc=1, device_id=((chan + dy) % 4, me), device_id_type=MESH
        )
    reads = []
    for c in range(CUT):
        span = pl.ds(c * PIECE, PIECE)
        reads.append(pltpu.make_async_copy(volt.at[:, span], held.at[:, span], held_sem.at[c]))
        reads[-1].start()
    loads = [
        pltpu.make_async_copy(first_in, first, local_sem.at[0]),
        pltpu.make_async_copy(turns_in, turns, local_sem.at[1]),
        pltpu.make_async_copy(
            phase.at[:, pl.ds(pl.multiple_of(chan * CHD, CHD), CHD), :], bins, local_sem.at[2]
        ),
        pltpu.make_async_copy(second_in, second, local_sem.at[3]),
        pltpu.make_async_copy(avg_in, avg, local_sem.at[4]),
        pltpu.make_async_copy(beam_in, beam, local_sem.at[5]),
    ]
    for load in loads:
        load.start()

    def arrange(i, carry):
        real = held[0, i].astype(F32)
        imag = held[1, i].astype(F32)
        real0, real1 = halves(real[:8], real[8:])
        imag0, imag1 = halves(imag[:8], imag[8:])
        for h, tile in enumerate(((real0, imag0), (real1, imag1))):
            tile = jnp.concatenate(tile, axis=0).astype(BF16)
            for d in range(BLK):
                sent[h, d, i] = tile[:, d * TD : (d + 1) * TD]
        return carry

    def send(h, c):
        for route in routes():
            there = towards(route)
            pltpu.make_async_remote_copy(
                src_ref=sent.at[h, there, pl.ds(c * PIECE, PIECE)],
                dst_ref=recv.at[h, me, pl.ds(c * PIECE, PIECE)],
                send_sem=send_sem,
                recv_sem=recv_sem.at[h * CUT + c],
                device_id=(chan, there),
                device_id_type=MESH,
            ).start()

    for c in range(CUT):
        reads[c].wait()
        lax.fori_loop(c * PIECE, (c + 1) * PIECE, arrange, 0)
        if c == 0:
            pl.semaphore_wait(barrier, 34)
        send(0, c)
    own = pltpu.make_async_copy(sent.at[:, me], recv.at[:, me], local_sem.at[6])
    own.start()

    def send_later(c, carry):
        send(1, c)
        return carry

    lax.fori_loop(0, CUT, send_later, 0)

    loads[2].wait()

    def digits(q, carry):
        top0, top1 = halves(bins[q], bins[q + 4])
        bottom0, bottom1 = halves(bins[q + 8], bins[q + 12])
        for h, tile in enumerate(((top0, bottom0), (top1, bottom1))):
            tile = jnp.concatenate(tile, axis=0)
            high[h, q] = (tile >> 4).astype(F32).astype(BF16)
            low[h, q] = (tile & 15).astype(F32).astype(BF16)
        return carry

    lax.fori_loop(0, NQ, digits, 0)
    acc[...] = jnp.zeros_like(acc)
    grid[...] = jnp.zeros_like(grid)
    for load in loads[:2] + loads[3:]:
        load.wait()
    own.wait()

    def sections(h):
        turn[...] = turns[2:]

        def section(i, carry):
            operand = jnp.concatenate(
                [recv[h, :, 2 * i + e].reshape(512, TD) for e in range(2)], axis=1
            )
            result = jnp.dot(first[...], operand, preferred_element_type=F32)
            for e in range(2):
                value = result[:, e * TD : (e + 1) * TD].reshape(2, BLK, 8, TD)
                tr, ti = turn[0], turn[1]
                turned = (value[0] * tr - value[1] * ti, value[0] * ti + value[1] * tr)
                mid[:, 2 * i + e] = jnp.concatenate(turned, axis=1).astype(BF16)
                sr, si = turns[0], turns[1]
                turn[0] = tr * sr - ti * si
                turn[1] = tr * si + ti * sr
            return carry

        for c in range(CUT):
            span = recv.at[h, pl.ds(0, BLK - 1), pl.ds(c * PIECE, PIECE)]
            pltpu.make_async_copy(span, span, recv_sem.at[h * CUT + c]).wait()
            lax.fori_loop(c * PIECE // 2, (c + 1) * PIECE // 2, section, 0)

    def forms(h):
        def form(j, carry):
            operand = jnp.concatenate(
                [mid[4 * j + b].reshape(256, TD) for b in range(4)], axis=1
            )
            result = jnp.dot(second[...], operand, preferred_element_type=F32)
            power = result[:128] * result[:128] + result[128:] * result[128:]
            for b in range(4):
                place = pl.multiple_of(8 + (4 * j + b) * 128, 8)
                det[pl.ds(place, 128), :] = power[:, b * TD : (b + 1) * TD]
            acc[h, j // 4] += jnp.dot(power.astype(BF16), avg[j % 4], preferred_element_type=F32)
            return carry

        lax.fori_loop(0, BLK // 4, form, 0)

    upper_rows = lax.broadcasted_iota(jnp.int32, (8, TD), 0) >= 4

    def picks(h):
        def pick(d, carry):
            for q in range(NQ):
                found = []
                for n in range(4):
                    row = beam[d * PSR + 4 * n + q]
                    found.append(det[pl.ds(8 + 4 * row - 4 * (n % 2), 8), :])
                tile = [jnp.where(upper_rows, found[n + 1], found[n]) for n in (0, 2)]
                tracks[h, d, q] = jnp.concatenate(tile, axis=0).astype(BF16)
            return carry

        lax.fori_loop(0, BLK, pick, 0)
        rtracks[h, me] = tracks[h, me]

        def send_tracks(c, carry):
            for route in routes():
                there = towards(route)
                pltpu.make_async_remote_copy(
                    src_ref=tracks.at[h, there, pl.ds(c * PIECE2, PIECE2)],
                    dst_ref=rtracks.at[h, me, pl.ds(c * PIECE2, PIECE2)],
                    send_sem=send2_sem,
                    recv_sem=recv2_sem.at[h * CUT2 + c],
                    device_id=(chan, there),
                    device_id_type=MESH,
                ).start()
            return carry

        lax.fori_loop(0, CUT2, send_tracks, 0)

    zero = jnp.zeros((16, TD), BF16)
    one = jnp.ones((16, TD), BF16)

    def folds(h, c):
        def fold(step, carry):
            q = step // 4
            s = step % 4
            left, right = [], []
            for e in range(8):
                series = rtracks[h, s * 8 + e, q]
                span = pl.ds(pl.multiple_of((s * 8 + e) * TD, TD), TD)
                low_now = low[h, q, :, span]
                high_now = high[h, q, :, span]
                left.append(
                    jnp.concatenate(
                        [jnp.where(low_now == v, series, zero) for v in range(16)], axis=0
                    )
                )
                right.append(
                    jnp.concatenate(
                        [jnp.where(high_now == v, one, zero) for v in range(16)], axis=0
                    )
                )
            grid[q] += lax.dot_general(
                jnp.concatenate(left, axis=1),
                jnp.concatenate(right, axis=1),
                (((1,), (1,)), ((), ())),
                preferred_element_type=F32,
            )
            return carry

        span = rtracks.at[h, pl.ds(0, BLK - 1), pl.ds(c * PIECE2, PIECE2)]
        pltpu.make_async_copy(span, span, recv2_sem.at[h * CUT2 + c]).wait()
        lax.fori_loop(c * PIECE2 * 4, (c + 1) * PIECE2 * 4, fold, 0)

    sections(0)
    forms(0)
    picks(0)
    sections(1)
    forms(1)
    picks(1)

    for g in range(2):
        both = [acc[h, g].T.reshape(16, SUMS, TD) for h in range(2)]
        inten[pl.ds(16 * g, 16)] = jnp.concatenate(both, axis=1).astype(BF16)
    rinten[me] = inten[me]
    for route in routes():
        there = towards(route)
        pltpu.make_async_remote_copy(
            src_ref=inten.at[there],
            dst_ref=rinten.at[me],
            send_sem=send3_sem,
            recv_sem=recv3_sem,
            device_id=(chan, there),
            device_id_type=MESH,
        ).start()

    for h in range(2):
        for c in range(CUT2):
            folds(h, c)

    same = (
        lax.broadcasted_iota(jnp.int32, (256, 256), 0) % 16
        == lax.broadcasted_iota(jnp.int32, (256, 256), 1) % 16
    )
    lane = lax.broadcasted_iota(jnp.int32, (1, 1, 256), 2)
    sub = lax.broadcasted_iota(jnp.int32, (2, 8, 256), 1)
    total = jnp.zeros((2, 8, 256), F32)
    for q in range(NQ):
        level = jnp.where(same, grid[q], 0.0).reshape(32, 8, 256)
        for d in (8, 4, 2, 1):
            count = 2 * d
            upper = (lane // d) % 2 == 1
            lower_part, upper_part = level[:count], level[count:]
            stay = jnp.where(upper, upper_part, lower_part)
            flat = jnp.where(upper, lower_part, upper_part).reshape(count * 8, 256)
            down = pltpu.roll(flat, d, 1).reshape(count, 8, 256)
            up = pltpu.roll(flat, 256 - d, 1).reshape(count, 8, 256)
            level = stay + jnp.where(upper, down, up)
        level = level + pltpu.roll(level, 6, 1)
        level = level + pltpu.roll(level, 7, 1)
        level = jnp.where(sub % 4 == 0, level, 0.0)
        total = total + (pltpu.roll(level, q, 1) if q else level)
    part[...] = total.reshape(PSR, NBIN) * (NBIN / (4 * CHD * float(TIME)))
    for dy in range(1, 4):
        pltpu.make_async_remote_copy(
            src_ref=part,
            dst_ref=parts.at[dy - 1],
            send_sem=send4_sem,
            recv_sem=recv4_sem.at[dy - 1],
            device_id=((chan + dy) % 4, me),
            device_id_type=MESH,
        ).start()

    span = rinten.at[pl.ds(0, BLK - 1)]
    pltpu.make_async_copy(span, span, recv3_sem).wait()
    averages = rinten[...].astype(F32)
    sides = [
        averages[:, h * SUMS : (h + 1) * SUMS].reshape(256, TD).T.reshape(16, 8, 256)
        for h in range(2)
    ]
    even, odd = halves(*sides)
    inten_out[...] = jnp.stack([even, odd], axis=1).reshape(BLK, CHD, 256)
    for dy in range(1, 4):
        pltpu.make_async_copy(part, parts.at[dy - 1], recv4_sem.at[dy - 1]).wait()
    folded_out[...] = part[...] + parts[0] + parts[1] + parts[2]

    span = recv.at[:, pl.ds(0, BLK - 1)]
    pltpu.make_async_copy(span, span, send_sem).wait()
    span = rtracks.at[:, pl.ds(0, BLK - 1)]
    pltpu.make_async_copy(span, span, send2_sem).wait()
    span = rinten.at[pl.ds(0, BLK - 1)]
    pltpu.make_async_copy(span, span, send3_sem).wait()
    pltpu.make_async_copy(parts, parts, send4_sem).wait()


def shards(volt, pulsar_beam, phase_bin):
    first, second, turns, avg = tables()
    far = pl.BlockSpec(memory_space=pltpu.HBM)
    whole = pl.BlockSpec(memory_space=pltpu.VMEM)
    dma = pltpu.SemaphoreType.DMA
    return pl.pallas_call(
        kernel,
        out_shape=(
            jax.ShapeDtypeStruct((BLK, CHD, TIME // DS), F32),
            jax.ShapeDtypeStruct((PSR, NBIN), F32),
        ),
        in_specs=[far] * 7,
        out_specs=(whole, whole),
        scratch_shapes=[
            pltpu.VMEM((2, PAIRS, 16, TIME), BF16),
            pltpu.VMEM((2, BLK, PAIRS, 16, TD), BF16),
            pltpu.VMEM((2, BLK, PAIRS, 16, TD), BF16),
            pltpu.VMEM((BLK, PAIRS, 16, TD), BF16),
            pltpu.VMEM((8 + 4 * F + 8, TD), F32),
            pltpu.VMEM((2, BLK, NQ, 16, TD), BF16),
            pltpu.VMEM((2, BLK, NQ, 16, TD), BF16),
            pltpu.VMEM((BLK, 2 * SUMS, TD), BF16),
            pltpu.VMEM((BLK, 2 * SUMS, TD), BF16),
            pltpu.VMEM((2, 2, TD, TD), F32),
            pltpu.VMEM((PSR, CHD, TIME), jnp.int32),
            pltpu.VMEM((2, NQ, 16, TIME), BF16),
            pltpu.VMEM((2, NQ, 16, TIME), BF16),
            pltpu.VMEM((NQ, 256, 256), F32),
            pltpu.VMEM((PSR, NBIN), F32),
            pltpu.VMEM((3, PSR, NBIN), F32),
            pltpu.VMEM((512, 512), BF16),
            pltpu.VMEM((256, 256), BF16),
            pltpu.VMEM((4, BLK, 8, TD), F32),
            pltpu.VMEM((4, 4 * TD, TD), BF16),
            pltpu.VMEM((2, BLK, 8, TD), F32),
            pltpu.SMEM((512,), jnp.int32),
            dma((7,)),
            dma((CUT,)),
            dma(()),
            dma((2 * CUT,)),
            dma(()),
            dma((2 * CUT2,)),
            dma(()),
            dma(()),
            dma(()),
            dma((3,)),
        ],
        compiler_params=pltpu.CompilerParams(
            collective_id=0, has_side_effects=True, vmem_limit_bytes=64 * 1024 * 1024
        ),
        name="beams",
    )(
        volt.reshape(2, PAIRS, 16, TIME),
        pulsar_beam,
        phase_bin,
        jnp.asarray(first),
        jnp.asarray(second),
        jnp.asarray(turns),
        jnp.asarray(avg),
    )


def solution(mesh):
    placed = (P(None, "feed", "chan", None), P(), P("feed", None, None))
    return jax.shard_map(
        shards,
        mesh=mesh,
        in_specs=placed,
        out_specs=(P("feed", "chan", None), P("feed", None)),
        check_vma=False,
    )
```

time: 95.6 us -> 82.4 us (0.86)
  Pallas kernels: 88.6 us -> 78.6 us
  local copies, waits for them, and re-layouts: 6.06 us -> 2.99 us
    pallas_call x1, Pallas kernels: 88.6 us -> 78.6 us  [shards(): pl.pallas_call(kernel, out_shape=(jax.ShapeDtypeStruct((BLK, CHD, TIME //...]
    unnamed x12 -> x2, local copies, waits for them, and re-layouts: 6.06 us -> 2.99 us
where the time goes in v2:
time: 82.4 us; the launch traced here: 82.2 us
  Pallas kernels  78.6 us (95%)
  local copies, waits for them, and re-layouts  2.99 us (4%)
    pallas_call x1, Pallas kernels, shards(): pl.pallas_call(kernel, out_shape=(jax.ShapeDtypeStruct((BLK, CHD, TIME //...  78.6 us
    unnamed x2, local copies, waits for them, and re-layouts  2.99 us

profile of v2, /device:TPU:1, one launch (start us, length us, event | category | flops | bytes accessed | tf_op | source)
XLA Modules:
  0.0 82.2 jit_solution(15609562924389435494)
XLA Ops:
  0.6 78.6 %beams.1 = (f32[32,8,256]{2,1,0:T(8,128)}, f32[16,256]{1,0:T(8,128)}) custom-call(bf16[2,16,16,4096]{3,2,1,0:T(8,128)(2,1)} %bitcast.1, s32[512]{0:T(512)} %beam_in.1, s32[16,32,4096]{2,1,0:T(8,128)} %phase.1, bf16[512,512]{1,0:T(8,128)(2,1)} %constant.8.clone.first_in, bf16[256,256]{1,0:T(8,128)(2,1)} %constant.9.clone.second_in, ...), custom_call_target="tpu_custom_call" | custom-call | tf_op jit(solution)/shard_map/beams/pallas_call | solution.py:410
  79.2 1.7 %copy.11 = f32[32,8,256]{2,1,0:T(8,128)} copy(f32[32,8,256]{2,1,0:T(8,128)} %get-tuple-element.4) | data formatting | bytes 524288
  80.9 1.3 %copy.12 = f32[16,256]{1,0:T(8,128)} copy(f32[16,256]{1,0:T(8,128)} %get-tuple-element.5) | data formatting | bytes 32768

commit v3 on v2

--- a/solution.py
+++ b/solution.py
@@ -19,10 +19,12 @@
 PSR = 16
 NQ = 4
 PAIRS = 16
-CUT = 4
-PIECE = PAIRS // CUT
-CUT2 = 2
-PIECE2 = NQ // CUT2
+PIECES = (((0, 2), (2, 2), (4, 4), (8, 4), (12, 4)), ((0, 4), (4, 4), (8, 4), (12, 2), (14, 2)))
+CUT = 5
+HOLD = 4
+WIDE = 16
+STEPS = BLK // WIDE
+CHUNKS = (((0, 4),), ((0, 2), (2, 2)))
 SUMS = TD // DS
 MESH = pl.DeviceIdType.MESH
 F32 = jnp.float32
@@ -102,8 +104,8 @@
     rinten,
     acc,
     bins,
-    high,
     low,
+    right,
     grid,
     part,
     parts,
@@ -144,8 +146,8 @@
             barrier, inc=1, device_id=((chan + dy) % 4, me), device_id_type=MESH
         )
     reads = []
-    for c in range(CUT):
-        span = pl.ds(c * PIECE, PIECE)
+    for c, piece in enumerate(PIECES[0]):
+        span = pl.ds(*piece)
         reads.append(pltpu.make_async_copy(volt.at[:, span], held.at[:, span], held_sem.at[c]))
         reads[-1].start()
     loads = [
@@ -172,52 +174,69 @@
                 sent[h, d, i] = tile[:, d * TD : (d + 1) * TD]
         return carry
 
-    def send(h, c):
+    def send(h, c, first_pair, count):
         for route in routes():
             there = towards(route)
             pltpu.make_async_remote_copy(
-                src_ref=sent.at[h, there, pl.ds(c * PIECE, PIECE)],
-                dst_ref=recv.at[h, me, pl.ds(c * PIECE, PIECE)],
+                src_ref=sent.at[h, there, pl.ds(first_pair, count)],
+                dst_ref=recv.at[h, me, pl.ds(first_pair, count)],
                 send_sem=send_sem,
                 recv_sem=recv_sem.at[h * CUT + c],
                 device_id=(chan, there),
                 device_id_type=MESH,
             ).start()
 
-    for c in range(CUT):
+    for c, (first_pair, count) in enumerate(PIECES[0]):
         reads[c].wait()
-        lax.fori_loop(c * PIECE, (c + 1) * PIECE, arrange, 0)
+        lax.fori_loop(first_pair, first_pair + count, arrange, 0)
         if c == 0:
             pl.semaphore_wait(barrier, 34)
-        send(0, c)
+        send(0, c, first_pair, count)
     own = pltpu.make_async_copy(sent.at[:, me], recv.at[:, me], local_sem.at[6])
     own.start()
 
     def send_later(c, carry):
-        send(1, c)
+        send(1, c, c * 4, 4)
         return carry
 
-    lax.fori_loop(0, CUT, send_later, 0)
-
+    lax.fori_loop(0, 3, send_later, 0)
+    send(1, 3, 12, 2)
+    send(1, 4, 14, 2)
+
+    zero = jnp.zeros((16, TD), BF16)
+    one = jnp.ones((16, TD), BF16)
     loads[2].wait()
 
-    def digits(q, carry):
-        top0, top1 = halves(bins[q], bins[q + 4])
-        bottom0, bottom1 = halves(bins[q + 8], bins[q + 12])
+    def digits(step, carry):
+        q = step // 4
+        span = pl.ds(pl.multiple_of(step % 4 * 8 * TD, 8 * TD), 8 * TD)
+        top0, top1 = halves(bins[q, :, span], bins[q + 4, :, span])
+        bottom0, bottom1 = halves(bins[q + 8, :, span], bins[q + 12, :, span])
         for h, tile in enumerate(((top0, bottom0), (top1, bottom1))):
             tile = jnp.concatenate(tile, axis=0)
-            high[h, q] = (tile >> 4).astype(F32).astype(BF16)
-            low[h, q] = (tile & 15).astype(F32).astype(BF16)
+            low[h, q, :, span] = (tile & 15).astype(F32).astype(BF16)
+            high = (tile >> 4).astype(F32).astype(BF16)
+            marks = [
+                jnp.concatenate(
+                    [
+                        jnp.where(high[:, e * TD : (e + 1) * TD] == v, one, zero)
+                        for v in range(16)
+                    ],
+                    axis=0,
+                )
+                for e in range(8)
+            ]
+            right[h, q, span, :] = jnp.concatenate(marks, axis=1).T
         return carry
 
-    lax.fori_loop(0, NQ, digits, 0)
+    lax.fori_loop(0, 4 * NQ, digits, 0)
     acc[...] = jnp.zeros_like(acc)
     grid[...] = jnp.zeros_like(grid)
     for load in loads[:2] + loads[3:]:
         load.wait()
     own.wait()
 
-    def sections(h):
+    def sections(h, before=None, then=None):
         turn[...] = turns[2:]
 
         def section(i, carry):
@@ -235,10 +254,12 @@
                 turn[1] = tr * si + ti * sr
             return carry
 
-        for c in range(CUT):
-            span = recv.at[h, pl.ds(0, BLK - 1), pl.ds(c * PIECE, PIECE)]
+        for c, (first_pair, count) in enumerate(PIECES[h]):
+            if c == before:
+                then()
+            span = recv.at[h, pl.ds(0, BLK - 1), pl.ds(first_pair, count)]
             pltpu.make_async_copy(span, span, recv_sem.at[h * CUT + c]).wait()
-            lax.fori_loop(c * PIECE // 2, (c + 1) * PIECE // 2, section, 0)
+            lax.fori_loop(first_pair // 2, (first_pair + count) // 2, section, 0)
 
     def forms(h):
         def form(j, carry):
@@ -271,62 +292,49 @@
         lax.fori_loop(0, BLK, pick, 0)
         rtracks[h, me] = tracks[h, me]
 
-        def send_tracks(c, carry):
+    def send_tracks(h):
+        for c, (first_group, count) in enumerate(CHUNKS[h]):
             for route in routes():
                 there = towards(route)
                 pltpu.make_async_remote_copy(
-                    src_ref=tracks.at[h, there, pl.ds(c * PIECE2, PIECE2)],
-                    dst_ref=rtracks.at[h, me, pl.ds(c * PIECE2, PIECE2)],
+                    src_ref=tracks.at[h, there, pl.ds(first_group, count)],
+                    dst_ref=rtracks.at[h, me, pl.ds(first_group, count)],
                     send_sem=send2_sem,
-                    recv_sem=recv2_sem.at[h * CUT2 + c],
+                    recv_sem=recv2_sem.at[h + c],
                     device_id=(chan, there),
                     device_id_type=MESH,
                 ).start()
-            return carry
-
-        lax.fori_loop(0, CUT2, send_tracks, 0)
-
-    zero = jnp.zeros((16, TD), BF16)
-    one = jnp.ones((16, TD), BF16)
-
-    def folds(h, c):
+
+    def folds(h, c, first_group, count):
         def fold(step, carry):
-            q = step // 4
-            s = step % 4
-            left, right = [], []
-            for e in range(8):
-                series = rtracks[h, s * 8 + e, q]
-                span = pl.ds(pl.multiple_of((s * 8 + e) * TD, TD), TD)
-                low_now = low[h, q, :, span]
-                high_now = high[h, q, :, span]
+            q = step // STEPS
+            s = step % STEPS
+            left = []
+            for e in range(WIDE):
+                series = rtracks[h, s * WIDE + e, q]
+                low_now = low[h, q, :, pl.ds(pl.multiple_of((s * WIDE + e) * TD, TD), TD)]
                 left.append(
                     jnp.concatenate(
                         [jnp.where(low_now == v, series, zero) for v in range(16)], axis=0
                     )
                 )
-                right.append(
-                    jnp.concatenate(
-                        [jnp.where(high_now == v, one, zero) for v in range(16)], axis=0
-                    )
-                )
-            grid[q] += lax.dot_general(
-                jnp.concatenate(left, axis=1),
-                jnp.concatenate(right, axis=1),
-                (((1,), (1,)), ((), ())),
-                preferred_element_type=F32,
+            span = pl.ds(pl.multiple_of(s * WIDE * TD, WIDE * TD), WIDE * TD)
+            grid[q] += jnp.dot(
+                jnp.concatenate(left, axis=1), right[h, q, span, :], preferred_element_type=F32
             )
             return carry
 
-        span = rtracks.at[h, pl.ds(0, BLK - 1), pl.ds(c * PIECE2, PIECE2)]
-        pltpu.make_async_copy(span, span, recv2_sem.at[h * CUT2 + c]).wait()
-        lax.fori_loop(c * PIECE2 * 4, (c + 1) * PIECE2 * 4, fold, 0)
+        span = rtracks.at[h, pl.ds(0, BLK - 1), pl.ds(first_group, count)]
+        pltpu.make_async_copy(span, span, recv2_sem.at[h + c]).wait()
+        lax.fori_loop(first_group * STEPS, (first_group + count) * STEPS, fold, 0)
 
     sections(0)
     forms(0)
     picks(0)
-    sections(1)
+    sections(1, HOLD, lambda: send_tracks(0))
     forms(1)
     picks(1)
+    send_tracks(1)
 
     for g in range(2):
         both = [acc[h, g].T.reshape(16, SUMS, TD) for h in range(2)]
@@ -343,18 +351,14 @@
             device_id_type=MESH,
         ).start()
 
-    for h in range(2):
-        for c in range(CUT2):
-            folds(h, c)
-
     same = (
         lax.broadcasted_iota(jnp.int32, (256, 256), 0) % 16
         == lax.broadcasted_iota(jnp.int32, (256, 256), 1) % 16
     )
     lane = lax.broadcasted_iota(jnp.int32, (1, 1, 256), 2)
     sub = lax.broadcasted_iota(jnp.int32, (2, 8, 256), 1)
-    total = jnp.zeros((2, 8, 256), F32)
-    for q in range(NQ):
+
+    def profile(q):
         level = jnp.where(same, grid[q], 0.0).reshape(32, 8, 256)
         for d in (8, 4, 2, 1):
             count = 2 * d
@@ -368,7 +372,14 @@
         level = level + pltpu.roll(level, 6, 1)
         level = level + pltpu.roll(level, 7, 1)
         level = jnp.where(sub % 4 == 0, level, 0.0)
-        total = total + (pltpu.roll(level, q, 1) if q else level)
+        return pltpu.roll(level, q, 1) if q else level
+
+    folds(0, 0, 0, 4)
+    total = jnp.zeros((2, 8, 256), F32)
+    for c, (first_group, count) in enumerate(CHUNKS[1]):
+        folds(1, c, first_group, count)
+        for q in range(first_group, first_group + count):
+            total = total + profile(q)
     part[...] = total.reshape(PSR, NBIN) * (NBIN / (4 * CHD * float(TIME)))
     for dy in range(1, 4):
         pltpu.make_async_remote_copy(
@@ -428,7 +439,7 @@
             pltpu.VMEM((2, 2, TD, TD), F32),
             pltpu.VMEM((PSR, CHD, TIME), jnp.int32),
             pltpu.VMEM((2, NQ, 16, TIME), BF16),
-            pltpu.VMEM((2, NQ, 16, TIME), BF16),
+            pltpu.VMEM((2, NQ, TIME, 256), BF16),
             pltpu.VMEM((NQ, 256, 256), F32),
             pltpu.VMEM((PSR, NBIN), F32),
             pltpu.VMEM((3, PSR, NBIN), F32),
@@ -443,24 +454,29 @@
             dma(()),
             dma((2 * CUT,)),
             dma(()),
-            dma((2 * CUT2,)),
+            dma((3,)),
             dma(()),
             dma(()),
             dma(()),
             dma((3,)),
         ],
         compiler_params=pltpu.CompilerParams(
-            collective_id=0, has_side_effects=True, vmem_limit_bytes=64 * 1024 * 1024
+            collective_id=0, has_side_effects=True, vmem_limit_bytes=50 * 1024 * 1024
         ),
         name="beams",
     )(
-        volt.reshape(2, PAIRS, 16, TIME),
-        pulsar_beam,
-        phase_bin,
-        jnp.asarray(first),
-        jnp.asarray(second),
-        jnp.asarray(turns),
-        jnp.asarray(avg),
+        *(
+            pltpu.with_memory_space_constraint(operand, pltpu.HBM)
+            for operand in (
+                volt.reshape(2, PAIRS, 16, TIME),
+                pulsar_beam,
+                phase_bin,
+                jnp.asarray(first),
+                jnp.asarray(second),
+                jnp.asarray(turns),
+                jnp.asarray(avg),
+            )
+        )
     )
 
 

time: 82.4 us -> 77.4 us (0.939)
  Pallas kernels: 78.6 us -> 75.3 us
  local copies, waits for them, and re-layouts: 2.99 us -> 1.31 us
    pallas_call x1, Pallas kernels: 78.6 us -> 75.3 us  [shards(): pl.pallas_call(kernel, out_shape=(jax.ShapeDtypeStruct((BLK, CHD, TIME //...]
    unnamed x2, local copies, waits for them, and re-layouts: 2.99 us -> 1.31 us
where the time goes in v3:
time: 77.4 us; the launch traced here: 77.3 us
  Pallas kernels  75.3 us (97%)
  local copies, waits for them, and re-layouts  1.31 us (2%)
    pallas_call x1, Pallas kernels, shards(): pl.pallas_call(kernel, out_shape=(jax.ShapeDtypeStruct((BLK, CHD, TIME //...  75.3 us

profile of v3, /device:TPU:1, one launch (start us, length us, event | category | flops | bytes accessed | tf_op | source)
XLA Modules:
  0.0 77.3 jit_solution(8057835970837309395)
XLA Ops:
  0.6 75.3 %beams.1 = (f32[32,8,256]{2,1,0:T(8,128)S(1)}, f32[16,256]{1,0:T(8,128)S(1)}) custom-call(bf16[2,16,16,4096]{3,2,1,0:T(8,128)(2,1)} %bitcast.1, s32[512]{0:T(512)} %beam_in.1, s32[16,32,4096]{2,1,0:T(8,128)} %phase.1, bf16[512,512]{1,0:T(8,128)(2,1)} %constant.8.clone.first_in, bf16[256,256]{1,0:T(8,128)(2,1)} %constant.9.clone.second_in, ...), custom_call_target="tpu_custom_call" | custom-call | tf_op jit(solution)/shard_map/beams/pallas_call | solution.py:421
  76.0 0.7 copy.11
  76.7 0.6 copy.12

commit v4 on v3

--- a/solution.py
+++ b/solution.py
@@ -24,7 +24,7 @@
 HOLD = 4
 WIDE = 16
 STEPS = BLK // WIDE
-CHUNKS = (((0, 4),), ((0, 2), (2, 2)))
+CHUNKS = (((0, 4),), ((0, 2), (2, 1), (3, 1)))
 SUMS = TD // DS
 MESH = pl.DeviceIdType.MESH
 F32 = jnp.float32
@@ -274,7 +274,7 @@
             acc[h, j // 4] += jnp.dot(power.astype(BF16), avg[j % 4], preferred_element_type=F32)
             return carry
 
-        lax.fori_loop(0, BLK // 4, form, 0)
+        lax.fori_loop(0, BLK // 4, form, 0, unroll=2)
 
     upper_rows = lax.broadcasted_iota(jnp.int32, (8, TD), 0) >= 4
 
@@ -355,31 +355,33 @@
         lax.broadcasted_iota(jnp.int32, (256, 256), 0) % 16
         == lax.broadcasted_iota(jnp.int32, (256, 256), 1) % 16
     )
-    lane = lax.broadcasted_iota(jnp.int32, (1, 1, 256), 2)
+    lane = lax.broadcasted_iota(jnp.int32, (1, 1, 1, 256), 3)
     sub = lax.broadcasted_iota(jnp.int32, (2, 8, 256), 1)
 
-    def profile(q):
-        level = jnp.where(same, grid[q], 0.0).reshape(32, 8, 256)
+    def profile(first_group, count):
+        level = grid[pl.ds(first_group, count)]
+        level = jnp.where(same, level, 0.0).reshape(count, 32, 8, 256)
         for d in (8, 4, 2, 1):
-            count = 2 * d
             upper = (lane // d) % 2 == 1
-            lower_part, upper_part = level[:count], level[count:]
+            lower_part, upper_part = level[:, : 2 * d], level[:, 2 * d :]
             stay = jnp.where(upper, upper_part, lower_part)
-            flat = jnp.where(upper, lower_part, upper_part).reshape(count * 8, 256)
-            down = pltpu.roll(flat, d, 1).reshape(count, 8, 256)
-            up = pltpu.roll(flat, 256 - d, 1).reshape(count, 8, 256)
+            flat = jnp.where(upper, lower_part, upper_part).reshape(count * 2 * d * 8, 256)
+            down = pltpu.roll(flat, d, 1).reshape(count, 2 * d, 8, 256)
+            up = pltpu.roll(flat, 256 - d, 1).reshape(count, 2 * d, 8, 256)
             level = stay + jnp.where(upper, down, up)
-        level = level + pltpu.roll(level, 6, 1)
-        level = level + pltpu.roll(level, 7, 1)
-        level = jnp.where(sub % 4 == 0, level, 0.0)
-        return pltpu.roll(level, q, 1) if q else level
+        found = jnp.zeros((2, 8, 256), F32)
+        for q in range(count):
+            sums = level[q] + pltpu.roll(level[q], 6, 1)
+            sums = sums + pltpu.roll(sums, 7, 1)
+            sums = jnp.where(sub % 4 == 0, sums, 0.0)
+            found = found + (pltpu.roll(sums, first_group + q, 1) if first_group + q else sums)
+        return found
 
     folds(0, 0, 0, 4)
     total = jnp.zeros((2, 8, 256), F32)
     for c, (first_group, count) in enumerate(CHUNKS[1]):
         folds(1, c, first_group, count)
-        for q in range(first_group, first_group + count):
-            total = total + profile(q)
+        total = total + profile(first_group, count)
     part[...] = total.reshape(PSR, NBIN) * (NBIN / (4 * CHD * float(TIME)))
     for dy in range(1, 4):
         pltpu.make_async_remote_copy(
@@ -454,7 +456,7 @@
             dma(()),
             dma((2 * CUT,)),
             dma(()),
-            dma((3,)),
+            dma((4,)),
             dma(()),
             dma(()),
             dma(()),

time: 77.4 us -> 77 us (level)
  no operation moved by 1% of the time
where the time goes in v4:
time: 77 us; the launch traced here: 76.8 us
  Pallas kernels  74.9 us (97%)
  local copies, waits for them, and re-layouts  1.31 us (2%)
    pallas_call x1, Pallas kernels, shards(): pl.pallas_call(kernel, out_shape=(jax.ShapeDtypeStruct((BLK, CHD, TIME //...  74.9 us

profile of v4, /device:TPU:1, one launch (start us, length us, event | category | flops | bytes accessed | tf_op | source)
XLA Modules:
  0.0 76.8 jit_solution(12455702495984126957)
XLA Ops:
  0.6 74.9 %beams.1 = (f32[32,8,256]{2,1,0:T(8,128)S(1)}, f32[16,256]{1,0:T(8,128)S(1)}) custom-call(bf16[2,16,16,4096]{3,2,1,0:T(8,128)(2,1)} %bitcast.1, s32[512]{0:T(512)} %beam_in.1, s32[16,32,4096]{2,1,0:T(8,128)} %phase.1, bf16[512,512]{1,0:T(8,128)(2,1)} %constant.8.clone.first_in, bf16[256,256]{1,0:T(8,128)(2,1)} %constant.9.clone.second_in, ...), custom_call_target="tpu_custom_call" | custom-call | tf_op jit(solution)/shard_map/beams/pallas_call | solution.py:423
  75.5 0.7 copy.11
  76.2 0.6 copy.12

commit v5 on v4

--- a/solution.py
+++ b/solution.py
@@ -62,16 +62,16 @@
 
 
 def routes():
-    hops = {0: 0, 1: 1, 3: 1, 2: 2}
-    found = [
-        (dz, dx, dc)
-        for dz in (0, 1, 3, 2)
-        for dx in (0, 1, 3, 2)
-        for dc in (0, 1)
-        if (dz, dx, dc) != (0, 0, 0)
-    ]
-    found.sort(key=lambda r: -(hops[r[0]] + hops[r[1]]))
-    return found
+    rings = (
+        ((2, 2),),
+        ((1, 2), (2, 1), (3, 2), (2, 3)),
+        ((1, 1), (3, 1), (3, 3), (1, 3)),
+        ((2, 0), (0, 2)),
+        ((1, 0), (0, 1), (3, 0), (0, 3)),
+        ((0, 0),),
+    )
+    found = [(dz, dx, dc) for ring in rings for dc in (0, 1) for dz, dx in ring]
+    return [route for route in found if route != (0, 0, 0)]
 
 
 def halves(low_rows, high_rows):
@@ -136,6 +136,11 @@
         dz, dx, dc = route
         return (((z + dz) % 4) * 4 + (x + dx) % 4) * 2 + (core + dc) % 2
 
+    reads = []
+    for c, piece in enumerate(PIECES[0]):
+        span = pl.ds(*piece)
+        reads.append(pltpu.make_async_copy(volt.at[:, span], held.at[:, span], held_sem.at[c]))
+        reads[-1].start()
     barrier = pltpu.get_barrier_semaphore()
     for route in routes():
         pl.semaphore_signal(
@@ -145,11 +150,6 @@
         pl.semaphore_signal(
             barrier, inc=1, device_id=((chan + dy) % 4, me), device_id_type=MESH
         )
-    reads = []
-    for c, piece in enumerate(PIECES[0]):
-        span = pl.ds(*piece)
-        reads.append(pltpu.make_async_copy(volt.at[:, span], held.at[:, span], held_sem.at[c]))
-        reads[-1].start()
     loads = [
         pltpu.make_async_copy(first_in, first, local_sem.at[0]),
         pltpu.make_async_copy(turns_in, turns, local_sem.at[1]),
@@ -383,7 +383,7 @@
         folds(1, c, first_group, count)
         total = total + profile(first_group, count)
     part[...] = total.reshape(PSR, NBIN) * (NBIN / (4 * CHD * float(TIME)))
-    for dy in range(1, 4):
+    for dy in (2, 1, 3):
         pltpu.make_async_remote_copy(
             src_ref=part,
             dst_ref=parts.at[dy - 1],

time: 77 us -> 76.7 us (level)
  no operation moved by 1% of the time
where the time goes in v5:
time: 76.7 us; the launch traced here: 76.6 us
  Pallas kernels  74.6 us (97%)
  local copies, waits for them, and re-layouts  1.31 us (2%)
    pallas_call x1, Pallas kernels, shards(): pl.pallas_call(kernel, out_shape=(jax.ShapeDtypeStruct((BLK, CHD, TIME //...  74.6 us

profile of v5, /device:TPU:1, one launch (start us, length us, event | category | flops | bytes accessed | tf_op | source)
XLA Modules:
  0.0 76.6 jit_solution(1932886988790698287)
XLA Ops:
  0.6 74.6 %beams.1 = (f32[32,8,256]{2,1,0:T(8,128)S(1)}, f32[16,256]{1,0:T(8,128)S(1)}) custom-call(bf16[2,16,16,4096]{3,2,1,0:T(8,128)(2,1)} %bitcast.1, s32[512]{0:T(512)} %beam_in.1, s32[16,32,4096]{2,1,0:T(8,128)} %phase.1, bf16[512,512]{1,0:T(8,128)(2,1)} %constant.8.clone.first_in, bf16[256,256]{1,0:T(8,128)(2,1)} %constant.9.clone.second_in, ...), custom_call_target="tpu_custom_call" | custom-call | tf_op jit(solution)/shard_map/beams/pallas_call | solution.py:423
  75.3 0.7 copy.11
  76.0 0.6 copy.12

commit v6 on v5

--- a/solution.py
+++ b/solution.py
@@ -289,7 +289,7 @@
                 tracks[h, d, q] = jnp.concatenate(tile, axis=0).astype(BF16)
             return carry
 
-        lax.fori_loop(0, BLK, pick, 0)
+        lax.fori_loop(0, BLK, pick, 0, unroll=4)
         rtracks[h, me] = tracks[h, me]
 
     def send_tracks(h):

time: 76.7 us -> 76.8 us (level)
  no operation moved by 1% of the time
where the time goes in v6:
time: 76.8 us; the launch traced here: 76.6 us
  Pallas kernels  74.7 us (97%)
  local copies, waits for them, and re-layouts  1.31 us (2%)
    pallas_call x1, Pallas kernels, shards(): pl.pallas_call(kernel, out_shape=(jax.ShapeDtypeStruct((BLK, CHD, TIME //...  74.7 us

profile of v6, /device:TPU:1, one launch (start us, length us, event | category | flops | bytes accessed | tf_op | source)
XLA Modules:
  0.0 76.6 jit_solution(16112049294400549103)
XLA Ops:
  0.6 74.7 %beams.1 = (f32[32,8,256]{2,1,0:T(8,128)S(1)}, f32[16,256]{1,0:T(8,128)S(1)}) custom-call(bf16[2,16,16,4096]{3,2,1,0:T(8,128)(2,1)} %bitcast.1, s32[512]{0:T(512)} %beam_in.1, s32[16,32,4096]{2,1,0:T(8,128)} %phase.1, bf16[512,512]{1,0:T(8,128)(2,1)} %constant.8.clone.first_in, bf16[256,256]{1,0:T(8,128)(2,1)} %constant.9.clone.second_in, ...), custom_call_target="tpu_custom_call" | custom-call | tf_op jit(solution)/shard_map/beams/pallas_call | solution.py:423
  75.3 0.7 copy.11
  76.0 0.6 copy.12
